TPU v7x, 512 devices: a whole 4x8x8 slice. The times are simulated.
512 devices in a mesh: blk: 32 (over y, x), row: 16 (over z, core).
Axes of the slice: x: 4, y: 8, z: 8, core: 2. Of those that a mesh axis runs over, the one named last changes fastest.
Arguments:
- snapshots: float32 [4096, 8192], P('row', 'blk'), may hold values from -20 to 20
Outputs:
- rotated: float32 [4096, 8192], P('row', 'blk')
All inputs are finite; a program needn't handle non-finite values.
Results may differ from a plain program's by a relative error of at most 0.00027.
Values sent between devices are 32-bit elements; how exact they have to be, the bound alone decides.
A program may use at most 64 MiB of HBM per device.

v0:
```python
import math

import jax
import jax.numpy as jnp
from jax import lax
from jax.sharding import PartitionSpec as P

NSTEPS = 5
ROUNDS = 2


def shifted(block, axis, distance):
    devices = range(lax.axis_size(axis))
    route = [(i - distance, i) for i in devices if i - distance in devices]
    return lax.ppermute(block, axis, route)


def finish_rotation(inverse_it, diagonal):
    inverse_root = lax.rsqrt(diagonal)
    return inverse_root[:, None] * inverse_it * (math.sqrt(0.5) * jnp.sqrt(diagonal))[None, :]


def full_solve(gram):
    pair_width = gram.shape[0]
    diagonal = jnp.diagonal(gram)
    inverse_root = lax.rsqrt(diagonal)
    scaled = gram * inverse_root[:, None] * inverse_root[None, :]
    identity = jnp.eye(pair_width, dtype=jnp.float32)
    forward_it = 0.5 * scaled
    inverse_it = identity
    for sweep_no in range(NSTEPS):
        factor = 1.5 * identity - 0.5 * jnp.dot(
            inverse_it, forward_it, precision=lax.Precision.HIGHEST
        )
        forward_it = jnp.dot(forward_it, factor, precision=lax.Precision.HIGHEST)
        inverse_it = jnp.dot(factor, inverse_it, precision=lax.Precision.HIGHEST)
    return finish_rotation(inverse_it, diagonal)


def rotate_pairs(column_pairs):
    local_gram = jnp.einsum(
        "rc,rd->cd", column_pairs, column_pairs, precision=lax.Precision.HIGHEST
    )
    gram = lax.psum(local_gram, "row")
    rotation = full_solve(gram)
    return jnp.dot(column_pairs, rotation, precision=lax.Precision.HIGHEST)


def move_blocks(column_pairs, position, blk_devices):
    block_width = column_pairs.shape[1] // 2
    upper_half = column_pairs[:, :block_width]
    lower_half = column_pairs[:, block_width:]
    rising = jnp.where(position == 0, lower_half, upper_half)
    arrived = shifted(rising, "blk", 1)
    falling = shifted(lower_half, "blk", -1)
    new_upper = jnp.where(position == 0, upper_half, arrived)
    new_lower = jnp.where(position == blk_devices - 1, upper_half, falling)
    return jnp.concatenate([new_upper, new_lower], axis=1)


def shards(snapshots):
    position = lax.axis_index("blk")
    blk_devices = lax.axis_size("blk")
    column_pairs = snapshots
    for round_no in range(ROUNDS):
        if round_no > 0:
            column_pairs = move_blocks(column_pairs, position, blk_devices)
        column_pairs = rotate_pairs(column_pairs)
    return column_pairs


def solution(mesh):
    placed = (P("row", "blk"),)
    return jax.shard_map(
        shards, mesh=mesh, in_specs=placed, out_specs=P("row", "blk"), check_vma=False
    )
```

profile of v0, /device:TPU:1, one launch (start us, length us, event | category | flops | bytes accessed | tf_op | source)
XLA Modules:
  0.0 282.9 jit_solution(8822160801611789170)
XLA Ops:
  6.5 0.9 copy-done
  7.5 1.3 fusion.36
  8.9 121.0 %all-reduce.3.cloned.1.call-done = f32[256,256]{1,0:T(8,128)} async-done(((f32[256,256]{1,0:T(8,128)}), f32[256,256]{1,0:T(8,128)}) %all-reduce.3.cloned.1.call-update) | async-done | bytes 262160 | tf_op jit(solution)/shard_map/psum | solution.py:44
  129.9 2.6 gather_fusion
  132.5 0.4 fusion.11
  133.2 0.4 fusion.14
  133.7 0.4 fusion.10
  134.1 0.4 fusion.38
  134.4 0.4 fusion.37
  134.8 0.4 fusion.9
  135.6 0.4 fusion.39
  136.0 0.4 fusion.8
  136.4 0.4 fusion.41
  137.1 0.4 fusion.7
  137.5 0.4 fusion.6
  137.9 0.6 convolution_bitcast_fusion
  138.5 3.1 %collective-permute-start = (f32[256,128]{0,1:T(8,128)S(1)}, f32[256,128]{0,1:T(8,128)S(1)}, u32[]{:S(2)}, u32[]{:S(2)}) collective-permute-start(f32[256,128]{0,1:T(8,128)S(1)} %get-tuple-element.7), channel_id=1, source_target_pairs={{0,16},{16,32},{32,48},{48,64},{64,80},{80,96},{96,112},{112,128},... | collective-permute-start | bytes 393224 | tf_op jit(solution)/shard_map/ppermute | solution.py:15
  141.7 1.5 collective-permute-start.1
  143.1 0.7 collective-permute-done
  143.8 3.5 %collective-permute-done.1 = f32[256,128]{0,1:T(8,128)S(1)} collective-permute-done((f32[256,128]{0,1:T(8,128)S(1)}, f32[256,128]{0,1:T(8,128)S(1)}, u32[]{:S(2)}, u32[]{:S(2)}) %collective-permute-start.1) | collective-permute-done | bytes 131104 | tf_op jit(solution)/shard_map/ppermute | solution.py:15
  147.4 1.1 fusion.17
  148.5 118.2 %all-reduce.5.cloned.1.call-done = f32[256,256]{1,0:T(8,128)} async-done(((f32[256,256]{1,0:T(8,128)}), f32[256,256]{1,0:T(8,128)}) %all-reduce.5.cloned.1.call-update) | async-done | bytes 262160 | tf_op jit(solution)/shard_map/psum | solution.py:44
  266.8 2.6 gather_fusion.1
  269.4 0.4 fusion.5
  270.1 0.4 fusion.15
  270.5 0.4 fusion.4
  270.9 0.4 fusion.44
  271.7 0.4 fusion.3
  272.8 0.4 fusion.2
  274.0 0.4 fusion.1
  274.4 0.4 fusion
  274.8 1.3 fusion.16
  (23 shorter events, 3.3 us)
Async XLA Ops:
  6.5 1.0 copy-start
  6.5 123.4 %all-reduce.3.cloned.1.call-start = ((), (), s32[]{:S(2)}) async-start(), calls=%async_computation | async-start | bytes 524288 | tf_op jit(solution)/shard_map/psum | solution.py:44
  8.8 257.9 %all-reduce.5.cloned.1.call-start = ((), (), s32[]{:S(2)}) async-start(), calls=%async_computation.1 | async-start | bytes 524288 | tf_op jit(solution)/shard_map/psum | solution.py:44
  129.9 2.7 copy-start.1
  138.5 5.3 %collective-permute-start = (f32[256,128]{0,1:T(8,128)S(1)}, f32[256,128]{0,1:T(8,128)S(1)}, u32[]{:S(2)}, u32[]{:S(2)}) collective-permute-start(f32[256,128]{0,1:T(8,128)S(1)} %get-tuple-element.7), channel_id=1, source_target_pairs={{0,16},{16,32},{32,48},{48,64},{64,80},{80,96},{96,112},{112,128},... | collective-permute-start | bytes 393224 | tf_op jit(solution)/shard_map/ppermute | solution.py:15
  141.7 5.7 %collective-permute-start.1 = (f32[256,128]{0,1:T(8,128)S(1)}, f32[256,128]{0,1:T(8,128)S(1)}, u32[]{:S(2)}, u32[]{:S(2)}) collective-permute-start(f32[256,128]{0,1:T(8,128)S(1)} %get-tuple-element.8), channel_id=1, source_target_pairs={{16,0},{32,16},{48,32},{64,48},{80,64},{96,80},{112,96},{128,112},... | collective-permute-start | bytes 393224 | tf_op jit(solution)/shard_map/ppermute | solution.py:15
  266.8 2.7 copy-start.2
Sparse Core Ops, SparseCore 0:
  9.7 120.1 all-reduce.2
  148.7 118.0 all-reduce.4
where the time goes:
time: 283 us
  waiting for transfers between devices  243 us (86%)
  matrix products  14.8 us (5%)
  between operations  13.7 us (5%)
  local copies, waits for them, and re-layouts  6.23 us (2%)
  starting transfers between devices  4.62 us (2%)
    psum x2, waiting for transfers between devices, rotate_pairs(): gram = lax.psum(local_gram, 'row')  239 us
  transfers between devices with their start and end apart: 4, of which 4 were waited for; matrix products, arithmetic and copies ran while one was open for 0% of the time, Pallas kernels for 0%

commit v1 on v0

v1 whole, which is shorter than its diff:
```python
import functools
import math

import jax
import jax.numpy as jnp
from jax import lax
from jax.experimental import pallas as pl
from jax.experimental.pallas import tpu as pltpu
from jax.sharding import PartitionSpec as P

NSTEPS = 5
MESH = pl.DeviceIdType.MESH


def product(a, b, lhs_dim=1):
    return lax.dot_general(
        a, b, (((lhs_dim,), (0,)), ((), ())), preferred_element_type=jnp.float32
    )


def split(a):
    high = a.astype(jnp.bfloat16)
    return high, (a - high.astype(jnp.float32)).astype(jnp.bfloat16)


def dot3(a, b, lhs_dim=1):
    return product(a[0], b[0], lhs_dim) + (
        product(a[0], b[1], lhs_dim) + product(a[1], b[0], lhs_dim)
    )


def eye(n):
    rows = lax.broadcasted_iota(jnp.int32, (n, n), 0)
    columns = lax.broadcasted_iota(jnp.int32, (n, n), 1)
    return rows == columns


def diagonals(a):
    kept = jnp.where(eye(a.shape[0]), a, 0.0)
    return jnp.sum(kept, axis=1, keepdims=True), jnp.sum(kept, axis=0, keepdims=True)


def newton_schulz(starts, last):
    n = starts[0].shape[0]
    scaled_eye = jnp.where(eye(n), 1.5, 0.0)
    ys = [split(0.5 * s) for s in starts]
    fs = [split(scaled_eye - 0.25 * s) for s in starts]
    zs = fs
    ys = [split(dot3(y, f)) for y, f in zip(ys, fs)]
    for step in range(1, NSTEPS):
        fs = [split(scaled_eye - 0.5 * dot3(z, y)) for z, y in zip(zs, ys)]
        if step == NSTEPS - 1:
            break
        ys, zs = (
            [split(dot3(y, f)) for y, f in zip(ys, fs)],
            [split(dot3(f, z)) for z, f in zip(zs, fs)],
        )
    return [last(n, f, y, z) for n, (f, y, z) in enumerate(zip(fs, ys, zs))]


def half_of(a, second, axis):
    n = a.shape[axis] // 2
    first = lax.slice_in_dim(a, 0, n, axis=axis)
    return jnp.where(second, lax.slice_in_dim(a, n, 2 * n, axis=axis), first)


def kernel(
    blk_devices, z_devices,
    x_ref, out_ref,
    moved, gram_local, gram_core, gram_sum, gram_parts, gram_shard, grams,
    cross_local, cross_core, cross_sum, cross_parts, cross_shard, cross,
    x_send, x_recv, gc_send, gc_recv, gz_send, gz_recv, ga_send, ga_recv, gf_send, gf_recv,
    cc_send, cc_recv, cz_send, cz_recv, ca_send, ca_recv, cf_send, cf_recv,
):
    k = lax.axis_index("blk")
    row = lax.axis_index("row")
    z = row // 2
    core = row % 2
    is_first = k == 0
    is_last = k == blk_devices - 1
    up = jnp.minimum(k + 1, blk_devices - 1)
    down = jnp.maximum(k - 1, 0)
    up_slot = jnp.where(is_last, 1, 0)
    down_slot = jnp.where(is_first, 0, 1)
    sibling = {"blk": k, "row": z * 2 + 1 - core}

    def peer(blk, t):
        return {"blk": blk, "row": lax.rem(z + t, z_devices) * 2 + core}

    def signal(device):
        pl.semaphore_signal(barrier, inc=1, device_id=device, device_id_type=MESH)

    def remote(src, dst, send, recv, device):
        return pltpu.make_async_remote_copy(
            src_ref=src, dst_ref=dst, send_sem=send, recv_sem=recv,
            device_id=device, device_id_type=MESH,
        )

    barrier = pltpu.get_barrier_semaphore()
    signal(sibling)
    for t in range(1, z_devices):
        signal(peer(k, t))

    @pl.when(jnp.logical_not(is_last))
    def _():
        for t in range(z_devices):
            signal(peer(up, t))

    @pl.when(jnp.logical_not(is_first))
    def _():
        for t in range(z_devices):
            signal(peer(down, t))

    x = x_ref[...]
    x_split = split(x)
    gram = dot3(x_split, x_split, 0)
    half_width = x.shape[1] // 2
    gram_local[:half_width] = gram[:half_width, :half_width]
    gram_local[half_width : 2 * half_width] = gram[:half_width, half_width:]
    gram_local[2 * half_width :] = gram[half_width:, half_width:]

    both = 1 - is_first.astype(jnp.int32) - is_last.astype(jnp.int32)
    pl.semaphore_wait(barrier, z_devices + z_devices + z_devices * both)

    g_half = gram_local.shape[0] // 2
    g_part = g_half // z_devices
    c_half = cross_local.shape[0] // 2
    c_part = c_half // z_devices

    def g_rows(which):
        return pl.ds(pl.multiple_of(which * g_half, 8), g_half)

    def c_rows(which):
        return pl.ds(pl.multiple_of(which * c_half, 8), c_half)

    gc = remote(gram_local.at[g_rows(1 - core)], gram_core, gc_send, gc_recv, sibling)
    gc.start()

    x_up = remote(x_ref, moved.at[up_slot], x_send.at[0], x_recv.at[up_slot], peer(up, 0))
    x_down = remote(x_ref, moved.at[down_slot], x_send.at[1], x_recv.at[down_slot], peer(down, 0))
    x_up_own = pltpu.make_async_copy(x_ref, moved.at[1], x_recv.at[1])
    x_down_own = pltpu.make_async_copy(x_ref, moved.at[0], x_recv.at[0])

    @pl.when(jnp.logical_not(is_last))
    def _():
        x_up.start()

    @pl.when(jnp.logical_not(is_first))
    def _():
        x_down.start()

    @pl.when(is_last)
    def _():
        x_up_own.start()

    @pl.when(is_first)
    def _():
        x_down_own.start()

    gc.wait_recv()
    gram_sum[...] = gram_local[g_rows(core)] + gram_core[...]

    gz = []
    for t in range(1, z_devices):
        there = lax.rem(z + t, z_devices)
        gz.append(
            remote(
                gram_sum.at[pl.ds(pl.multiple_of(there * g_part, 8), g_part)],
                gram_parts.at[t - 1], gz_send.at[t - 1], gz_recv.at[t - 1], peer(k, t),
            )
        )
        gz[-1].start()
    shard = gram_sum[pl.ds(pl.multiple_of(z * g_part, 8), g_part)]
    for t in range(1, z_devices):
        gz[t - 1].wait_recv()
        shard = shard + gram_parts[t - 1]
    gram_shard[...] = shard

    g_mine = pl.ds(pl.multiple_of(core * g_half + z * g_part, 8), g_part)
    ga_up = [
        remote(gram_shard, grams.at[up_slot, g_mine], ga_send.at[t], ga_recv.at[up_slot], peer(up, t))
        for t in range(z_devices)
    ]
    ga_down = [
        remote(
            gram_shard, grams.at[down_slot, g_mine],
            ga_send.at[z_devices + t], ga_recv.at[down_slot], peer(down, t),
        )
        for t in range(z_devices)
    ]
    ga_up_own = pltpu.make_async_copy(gram_shard, grams.at[1, g_mine], ga_recv.at[1])
    ga_down_own = pltpu.make_async_copy(gram_shard, grams.at[0, g_mine], ga_recv.at[0])

    @pl.when(jnp.logical_not(is_last))
    def _():
        ga_up[0].start()

    @pl.when(jnp.logical_not(is_first))
    def _():
        ga_down[0].start()

    @pl.when(is_last)
    def _():
        ga_up_own.start()

    @pl.when(is_first)
    def _():
        ga_down_own.start()

    for t in range(1, z_devices):
        ga_up[t].start()
        ga_down[t].start()

    for slot in range(2):
        pltpu.make_async_copy(moved.at[slot], moved.at[slot], x_recv.at[slot]).wait()
    a_split = split(moved[0])
    b_split = split(moved[1])
    cross_local[...] = dot3(a_split, b_split, 0)
    cc = remote(cross_local.at[c_rows(1 - core)], cross_core, cc_send, cc_recv, sibling)
    cc.start()
    cc.wait_recv()
    cross_sum[...] = cross_local[c_rows(core)] + cross_core[...]
    cz = []
    for t in range(1, z_devices):
        there = lax.rem(z + t, z_devices)
        cz.append(
            remote(
                cross_sum.at[pl.ds(pl.multiple_of(there * c_part, 8), c_part)],
                cross_parts.at[t - 1], cz_send.at[t - 1], cz_recv.at[t - 1], peer(k, t),
            )
        )
        cz[-1].start()

    gf = []
    for slot in range(2):
        here = grams.at[slot, g_rows(core)]
        pltpu.make_async_copy(here, here, ga_recv.at[slot]).wait()
        gf.append(remote(here, here, gf_send.at[slot], gf_recv.at[slot], sibling))
        gf[-1].start()

    shard = cross_sum[pl.ds(pl.multiple_of(z * c_part, 8), c_part)]
    for t in range(1, z_devices):
        cz[t - 1].wait_recv()
        shard = shard + cross_parts[t - 1]
    cross_shard[...] = shard
    c_mine = pl.ds(pl.multiple_of(core * c_half + z * c_part, 8), c_part)
    ca = []
    for t in range(1, z_devices):
        ca.append(
            remote(cross_shard, cross.at[c_mine], ca_send.at[t - 1], ca_recv.at[0], peer(k, t))
        )
        ca[-1].start()
    ca_own = pltpu.make_async_copy(cross_shard, cross.at[c_mine], ca_recv.at[0])
    ca_own.start()

    for slot in range(2):
        gf[slot].wait_recv()

    second = (k == 1, jnp.logical_not(is_last))
    diag_columns, diag_rows, roots_columns, scaled = [], [], [], []
    for slot in range(2):
        g = grams[slot]
        upper = g[half_width : 2 * half_width]
        full = jnp.concatenate(
            [
                jnp.concatenate([g[:half_width], upper], axis=1),
                jnp.concatenate([upper.T, g[2 * half_width :]], axis=1),
            ],
            axis=0,
        )
        column, line = diagonals(full)
        diag_columns.append(column)
        diag_rows.append(line)
        roots_columns.append(lax.rsqrt(column))
        scaled.append(full * roots_columns[slot] * lax.rsqrt(line))
    scaled_split = [split(s) for s in scaled]

    def end_first(slot, factor, y, z_now):
        z_half = [half_of(part.astype(jnp.float32), second[slot], 1).astype(jnp.bfloat16) for part in z_now]
        return dot3(factor, z_half)

    z_first = newton_schulz(scaled, end_first)
    z_split = [split(v) for v in z_first]
    own = [dot3(z_split[s], split(dot3(scaled_split[s], z_split[s])), 0) for s in range(2)]

    here = cross.at[c_rows(core)]
    pltpu.make_async_copy(here, here, ca_recv.at[0]).wait()
    cf = remote(here, here, cf_send, cf_recv, sibling)
    cf.start()
    cf.wait_recv()

    cross_scaled = cross[...] * roots_columns[0] * lax.rsqrt(diag_rows[1])
    between = dot3(z_split[0], split(dot3(split(cross_scaled), z_split[1])), 0)
    t_columns, t_rows = zip(*[diagonals(o) for o in own])
    it_columns = [lax.rsqrt(v) for v in t_columns]
    it_rows = [lax.rsqrt(v) for v in t_rows]
    off = between * it_columns[0] * it_rows[1]
    scaled2 = jnp.concatenate(
        [
            jnp.concatenate([own[0] * it_columns[0] * it_rows[0], off], axis=1),
            jnp.concatenate([off.T, own[1] * it_columns[1] * it_rows[1]], axis=1),
        ],
        axis=0,
    )
    (z_second,) = newton_schulz([scaled2], lambda n, factor, y, z_now: dot3(factor, z_now))

    diag2 = jnp.concatenate(
        [half_of(diag_rows[s], second[s], 1) * t_rows[s] for s in range(2)], axis=1
    )
    ends = math.sqrt(0.5) * jnp.sqrt(0.5 * diag2)
    result = None
    for s in range(2):
        mine = z_second[s * half_width : (s + 1) * half_width] * it_columns[s]
        both_rotations = roots_columns[s] * dot3(z_split[s], split(mine)) * ends
        term = dot3((a_split, b_split)[s], split(both_rotations))
        result = term if result is None else result + term
    out_ref[...] = result

    gc.wait_send()
    cc.wait_send()
    cf.wait_send()
    for copy in gz + cz + ca + gf + ga_up[1:] + ga_down[1:]:
        copy.wait_send()

    @pl.when(jnp.logical_not(is_last))
    def _():
        x_up.wait_send()
        ga_up[0].wait_send()

    @pl.when(jnp.logical_not(is_first))
    def _():
        x_down.wait_send()
        ga_down[0].wait_send()


def shards(blk_devices, z_devices, x):
    rows, width = x.shape
    half = width // 2
    dma = pltpu.SemaphoreType.DMA
    f32 = jnp.float32
    g_half, c_half = 3 * half // 2, width // 2
    vmem = pl.BlockSpec(memory_space=pltpu.VMEM)
    return pl.pallas_call(
        functools.partial(kernel, blk_devices, z_devices),
        out_shape=jax.ShapeDtypeStruct(x.shape, f32),
        in_specs=[vmem],
        out_specs=vmem,
        scratch_shapes=[
            pltpu.VMEM((2, rows, width), f32),
            pltpu.VMEM((3 * half, half), f32),
            pltpu.VMEM((g_half, half), f32),
            pltpu.VMEM((g_half, half), f32),
            pltpu.VMEM((z_devices - 1, g_half // z_devices, half), f32),
            pltpu.VMEM((g_half // z_devices, half), f32),
            pltpu.VMEM((2, 3 * half, half), f32),
            pltpu.VMEM((width, width), f32),
            pltpu.VMEM((c_half, width), f32),
            pltpu.VMEM((c_half, width), f32),
            pltpu.VMEM((z_devices - 1, c_half // z_devices, width), f32),
            pltpu.VMEM((c_half // z_devices, width), f32),
            pltpu.VMEM((width, width), f32),
            dma((2,)), dma((2,)), dma, dma,
            dma((z_devices - 1,)), dma((z_devices - 1,)), dma((2 * z_devices,)), dma((2,)),
            dma((2,)), dma((2,)), dma, dma,
            dma((z_devices - 1,)), dma((z_devices - 1,)), dma((z_devices - 1,)), dma((1,)),
            dma, dma,
        ],
        compiler_params=pltpu.CompilerParams(
            collective_id=0, has_side_effects=True, vmem_limit_bytes=32 * 1024 * 1024
        ),
        cost_estimate=pl.CostEstimate(
            flops=40 * 3 * 2 * width**3, bytes_accessed=8 * rows * width, transcendentals=4096
        ),
        name="rotate_pairs",
    )(x)


def solution(mesh):
    run = functools.partial(shards, mesh.shape["blk"], mesh.shape["row"] // 2)
    return jax.shard_map(
        run, mesh=mesh, in_specs=(P("row", "blk"),), out_specs=P("row", "blk"), check_vma=False
    )
```

time: 283 us -> 44.7 us (0.16)
  waiting for transfers between devices: 243 us -> 0 us
  Pallas kernels: 0 us -> 42.9 us
  matrix products: 14.8 us -> 0 us
  between operations: 13.7 us -> 0.01 us
  starting transfers between devices: 4.62 us -> 0 us
  local copies, waits for them, and re-layouts: 6.23 us -> 1.65 us
    psum x2 -> x0, waiting for transfers between devices: 239 us -> none  [rotate_pairs(): gram = lax.psum(local_gram, 'row')]
    pallas_call x0 -> x1, Pallas kernels: none -> 42.9 us  [shards(): pl.pallas_call(functools.partial(kernel, blk_devices, z_devices), out_sha...]
    dot_general x32 -> x0, matrix products: 14.8 us -> none  [the longest x10 3.83 us: full_solve(): jnp.dot(inverse_it, forward_it, precision=lax.Precision.HIGHEST)]
    gather x2 -> x0, local copies, waits for them, and re-layouts: 5.27 us -> none  [full_solve(): diagonal = jnp.diagonal(gram)]
    ppermute x2 -> x0, starting transfers between devices: 4.58 us -> none  [shifted(): return lax.ppermute(block, axis, route)]
    ppermute x2 -> x0, waiting for transfers between devices: 4.23 us -> none  [shifted(): return lax.ppermute(block, axis, route)]
  transfers between devices with their start and end apart: 4 -> 0, of which waited for: 4 -> 0; matrix products, arithmetic and copies ran while one was open for 0% -> 0% of each run, Pallas kernels for 0% -> 0%
where the time goes in v1:
time: 44.7 us; the launch traced here: 44.6 us
  Pallas kernels  42.9 us (96%)
  local copies, waits for them, and re-layouts  1.65 us (4%)
    pallas_call x1, Pallas kernels, shards(): pl.pallas_call(functools.partial(kernel, blk_devices, z_devices), out_sha...  42.9 us
    unnamed x3, local copies, waits for them, and re-layouts  1.65 us

profile of v1, /device:TPU:1, one launch (start us, length us, event | category | flops | bytes accessed | tf_op | source)
XLA Modules:
  0.0 44.6 jit_solution(1634817122188266578)
XLA Ops:
  0.0 0.0 copy-start
  0.0 0.9 %copy-done = f32[256,256]{1,0:T(8,128)S(1)} copy-done((f32[256,256]{1,0:T(8,128)S(1)}, f32[256,256]{1,0:T(8,128)}, u32[]{:S(2)}) %copy-start) | copy-done | bytes 262168
  1.0 42.9 %rotate_pairs.1 = f32[256,256]{1,0:T(8,128)S(1)} custom-call(f32[256,256]{1,0:T(8,128)S(1)} %copy-done), custom_call_target="tpu_custom_call" | custom-call | flops 4026531840 | bytes 524288 | tf_op jit(solution)/shard_map/rotate_pairs/pallas_call | solution.py:343
  43.9 0.7 %copy.3 = f32[256,256]{1,0:T(8,128)} copy(f32[256,256]{1,0:T(8,128)S(1)} %rotate_pairs.1) | data formatting | bytes 524288
Async XLA Ops:
  0.0 0.9 %copy-start = (f32[256,256]{1,0:T(8,128)S(1)}, f32[256,256]{1,0:T(8,128)}, u32[]{:S(2)}) copy-start(f32[256,256]{1,0:T(8,128)} %x_ref.1) | copy-start | bytes 786436

commit v2 on v0

v2 whole, which is shorter than its diff:
```python
import functools
import math

import jax
import jax.numpy as jnp
from jax import lax
from jax.experimental import pallas as pl
from jax.experimental.pallas import tpu as pltpu
from jax.sharding import PartitionSpec as P

NSTEPS = 5
MESH = pl.DeviceIdType.MESH


def product(a, b, lhs_dim=1):
    return lax.dot_general(
        a, b, (((lhs_dim,), (0,)), ((), ())), preferred_element_type=jnp.float32
    )


def split(a):
    high = a.astype(jnp.bfloat16)
    return high, (a - high.astype(jnp.float32)).astype(jnp.bfloat16)


def dot3(a, b, lhs_dim=1):
    return product(a[0], b[0], lhs_dim) + (
        product(a[0], b[1], lhs_dim) + product(a[1], b[0], lhs_dim)
    )


def eye(n):
    rows = lax.broadcasted_iota(jnp.int32, (n, n), 0)
    columns = lax.broadcasted_iota(jnp.int32, (n, n), 1)
    return rows == columns


def diagonals(a):
    kept = jnp.where(eye(a.shape[0]), a, 0.0)
    return jnp.sum(kept, axis=1, keepdims=True), jnp.sum(kept, axis=0, keepdims=True)


class Solve:
    def __init__(self, starts):
        self.eye = jnp.where(eye(starts[0].shape[0]), 1.5, 0.0)
        self.f = [split(self.eye - 0.25 * m) for m in starts]
        self.y = [dot3(split(0.5 * m), f) for m, f in zip(starts, self.f)]
        self.z = [self.eye - 0.25 * m for m in starts]
        self.z_split = self.f
        self.y_split = [split(y) for y in self.y]

    def factors(self):
        self.f = [split(self.eye - 0.5 * dot3(z, y)) for z, y in zip(self.z_split, self.y_split)]

    def step(self):
        self.factors()
        self.y = [dot3(y, f) for y, f in zip(self.y_split, self.f)]
        self.z = [dot3(f, z) for z, f in zip(self.z_split, self.f)]
        self.y_split = [split(y) for y in self.y]
        self.z_split = [split(z) for z in self.z]


def half_of(a, second, axis):
    n = a.shape[axis] // 2
    first = lax.slice_in_dim(a, 0, n, axis=axis)
    return jnp.where(second, lax.slice_in_dim(a, n, 2 * n, axis=axis), first)


def kernel(
    blk_devices, z_devices,
    x_hbm, out_ref,
    x_ref, moved, gram_local, gram_core, gram_sum, gram_parts, gram_full, grams,
    cross_local, cross_core, cross_sum, cross_parts, cross_shard, cross,
    load_sem, x_send, x_recv, gc_send, gc_recv, gz_send, gz_recv, ga_send, ga_recv, gx_send, gx_recv,
    cc_send, cc_recv, cz_send, cz_recv, ca_send, ca_recv, cf_send, cf_recv,
):
    k = lax.axis_index("blk")
    row = lax.axis_index("row")
    z = row // 2
    core = row % 2
    is_first = k == 0
    is_last = k == blk_devices - 1
    up = jnp.minimum(k + 1, blk_devices - 1)
    down = jnp.maximum(k - 1, 0)
    up_slot = jnp.where(is_last, 1, 0)
    down_slot = jnp.where(is_first, 0, 1)
    second = (k == 1, jnp.logical_not(is_last))
    half_width = x_ref.shape[1] // 2
    g_half = gram_local.shape[0] // 2
    g_part = g_half // z_devices
    c_half = cross_local.shape[0] // 2
    c_part = c_half // z_devices
    far_first = sorted(range(1, z_devices), key=lambda t: -min(t, z_devices - t))
    near_first = far_first[::-1]

    def peer(blk, t, other=False):
        return {"blk": blk, "row": lax.rem(z + t, z_devices) * 2 + (1 - core if other else core)}

    sibling = peer(k, 0, True)

    def remote(src, dst, send, recv, device):
        return pltpu.make_async_remote_copy(
            src_ref=src, dst_ref=dst, send_sem=send, recv_sem=recv,
            device_id=device, device_id_type=MESH,
        )

    def rows_at(start, size):
        return pl.ds(pl.multiple_of(start, 8), size)

    def either(condition, yes, no):
        pl.when(condition)(lambda: yes() and None)
        pl.when(jnp.logical_not(condition))(lambda: no() and None)

    load = pltpu.make_async_copy(x_hbm, x_ref, load_sem)
    load.start()

    barrier = pltpu.get_barrier_semaphore()

    def signal(device):
        pl.semaphore_signal(barrier, inc=1, device_id=device, device_id_type=MESH)

    for t in far_first:
        signal(peer(k, t))

    @pl.when(jnp.logical_not(is_last))
    def _():
        signal(peer(up, 0))
        signal(peer(up, 0, True))

    @pl.when(jnp.logical_not(is_first))
    def _():
        signal(peer(down, 0))
        signal(peer(down, 0, True))

    signal(sibling)

    load.wait()
    x_split = split(x_ref[...])
    g = dot3(x_split, x_split, 0)
    gram_local[:half_width] = g[:half_width, :half_width]
    gram_local[half_width : 2 * half_width] = g[:half_width, half_width:]
    gram_local[2 * half_width :] = g[half_width:, half_width:]

    neighbours = 2 - is_first.astype(jnp.int32) - is_last.astype(jnp.int32)
    pl.semaphore_wait(barrier, z_devices + 2 * neighbours)

    x_up = remote(x_ref, moved.at[up_slot], x_send.at[0], x_recv.at[up_slot], peer(up, 0))
    x_down = remote(x_ref, moved.at[down_slot], x_send.at[1], x_recv.at[down_slot], peer(down, 0))
    either(is_last, pltpu.make_async_copy(x_ref, moved.at[1], x_recv.at[1]).start, x_up.start)
    either(is_first, pltpu.make_async_copy(x_ref, moved.at[0], x_recv.at[0]).start, x_down.start)

    gc = remote(gram_local.at[rows_at((1 - core) * g_half, g_half)], gram_core, gc_send, gc_recv, sibling)
    gc.start()
    sent = [gc]

    def scatter(total, part, parts, send, recv):
        copies = {}
        for t in far_first:
            there = rows_at(lax.rem(z + t, z_devices) * part, part)
            copies[t] = remote(total.at[there], parts.at[t - 1], send.at[t - 1], recv.at[t - 1], peer(k, t))
            copies[t].start()
        sent.extend(copies.values())
        return copies

    def gather(total, part, parts, copies):
        shard = total[rows_at(z * part, part)]
        for t in near_first:
            copies[t].wait_recv()
            shard = shard + parts[t - 1]
        return shard

    gc.wait_recv()
    gram_sum[...] = gram_local[rows_at(core * g_half, g_half)] + gram_core[...]
    gz = scatter(gram_sum, g_part, gram_parts, gz_send, gz_recv)
    own_rows = rows_at(z * g_part, g_part)
    gram_full[own_rows] = gather(gram_sum, g_part, gram_parts, gz)
    ga = {}
    for t in far_first:
        ga[t] = remote(
            gram_full.at[own_rows], gram_full.at[own_rows], ga_send.at[t - 1], ga_recv.at[t - 1], peer(k, t)
        )
        ga[t].start()
    sent.extend(ga.values())

    forwarded = []

    def forward(t):
        from_z = lax.rem(z - t + z_devices, z_devices)
        src = gram_full.at[rows_at(from_z * g_part, g_part)]
        there = rows_at(core * g_half + from_z * g_part, g_part)
        if t:
            ga[t].wait_recv()
        for n, (edge, blk, slot, own_slot) in enumerate(((is_last, up, up_slot, 1), (is_first, down, down_slot, 0))):
            dst = grams.at[slot, there]
            straight = remote(src, dst, gx_send.at[2 * n, t], gx_recv.at[slot], peer(blk, 0))
            across = remote(src, dst, gx_send.at[2 * n + 1, t], gx_recv.at[slot], peer(blk, 0, True))
            stays = pltpu.make_async_copy(src, grams.at[own_slot, there], gx_recv.at[own_slot])
            across.start()
            either(edge, stays.start, straight.start)
            sent.append(across)
            forwarded.append((edge, straight))

    forward(0)

    for slot in range(2):
        pltpu.make_async_copy(moved.at[slot], moved.at[slot], x_recv.at[slot]).wait()
    moved_split = [split(moved[slot]) for slot in range(2)]
    cross_local[...] = dot3(*moved_split, 0)
    cc = remote(cross_local.at[rows_at((1 - core) * c_half, c_half)], cross_core, cc_send, cc_recv, sibling)
    cc.start()
    sent.append(cc)
    for t in near_first[:2]:
        forward(t)
    cc.wait_recv()
    cross_sum[...] = cross_local[rows_at(core * c_half, c_half)] + cross_core[...]
    cz = scatter(cross_sum, c_part, cross_parts, cz_send, cz_recv)
    for t in near_first[2:]:
        forward(t)

    for slot in range(2):
        pltpu.make_async_copy(grams.at[slot], grams.at[slot], gx_recv.at[slot]).wait()
    diag_rows, roots_columns, scaled = [], [], []
    for slot in range(2):
        g = grams[slot]
        upper = g[half_width : 2 * half_width]
        full = jnp.concatenate(
            [
                jnp.concatenate([g[:half_width], upper], axis=1),
                jnp.concatenate([upper.T, g[2 * half_width :]], axis=1),
            ],
            axis=0,
        )
        column, line = diagonals(full)
        diag_rows.append(line)
        roots_columns.append(lax.rsqrt(column))
        scaled.append(full * roots_columns[slot] * lax.rsqrt(line))
    first = Solve(scaled)
    first.step()

    cross_shard[...] = gather(cross_sum, c_part, cross_parts, cz)
    c_mine = rows_at(core * c_half + z * c_part, c_part)
    for t in far_first:
        ca = remote(cross_shard, cross.at[c_mine], ca_send.at[t - 1], ca_recv, peer(k, t))
        ca.start()
        sent.append(ca)
    pltpu.make_async_copy(cross_shard, cross.at[c_mine], ca_recv).start()

    for _ in range(NSTEPS - 3):
        first.step()
    first.factors()
    zs, t_rows, its, ul = [], [], [], []
    for n in range(2):
        z_half = dot3(first.f[n], split(half_of(first.z[n], second[n], 1)))
        y_half = dot3(first.f[n], split(half_of(first.y[n], second[n], 1)))
        own = 2.0 * dot3(split(z_half), split(y_half), 0)
        t_column, t_row = diagonals(own)
        it_row = lax.rsqrt(t_row)
        t_rows.append(t_row)
        z_unit = z_half * it_row
        zs.append(split(z_unit))
        its.append(own * lax.rsqrt(t_column) * it_row)
        ul.append(split(dot3(moved_split[n], split(z_unit * roots_columns[n]))))
    ul = [jnp.concatenate([ul[0][p], ul[1][p]], axis=1) for p in range(2)]
    diag2 = jnp.concatenate([half_of(diag_rows[n], second[n], 1) * t_rows[n] for n in range(2)], axis=1)
    ends = math.sqrt(0.5) * jnp.sqrt(0.5 * diag2)
    root_row = lax.rsqrt(diag_rows[1])

    here = cross.at[rows_at(core * c_half, c_half)]
    pltpu.make_async_copy(here, here, ca_recv).wait()
    cf = remote(here, here, cf_send, cf_recv, sibling)
    cf.start()
    sent.append(cf)
    cf.wait_recv()

    cross_scaled = cross[...] * roots_columns[0] * root_row
    off = dot3(zs[0], split(dot3(split(cross_scaled), zs[1])), 0)
    scaled2 = jnp.concatenate(
        [jnp.concatenate([its[0], off], axis=1), jnp.concatenate([off.T, its[1]], axis=1)], axis=0
    )
    last = Solve([scaled2])
    for _ in range(NSTEPS - 2):
        last.step()
    last.factors()
    almost = dot3(ul, last.z_split[0])
    out_ref[...] = dot3(split(almost), last.f[0]) * ends

    for copy in sent:
        copy.wait_send()
    for edge, copy in forwarded + [(is_last, x_up), (is_first, x_down)]:
        pl.when(jnp.logical_not(edge))(lambda copy=copy: copy.wait_send())


def shards(blk_devices, z_devices, x):
    rows, width = x.shape
    half = width // 2
    dma = pltpu.SemaphoreType.DMA
    g_half, c_half = 3 * half // 2, width // 2
    others = z_devices - 1
    vmem = lambda *shape: pltpu.VMEM(shape, jnp.float32)
    return pl.pallas_call(
        functools.partial(kernel, blk_devices, z_devices),
        out_shape=jax.ShapeDtypeStruct(x.shape, jnp.float32),
        in_specs=[pl.BlockSpec(memory_space=pltpu.MemorySpace.HBM)],
        out_specs=pl.BlockSpec(memory_space=pltpu.VMEM),
        scratch_shapes=[
            vmem(rows, width), vmem(2, rows, width),
            vmem(3 * half, half), vmem(g_half, half), vmem(g_half, half),
            vmem(others, g_half // z_devices, half), vmem(g_half, half), vmem(2, 3 * half, half),
            vmem(width, width), vmem(c_half, width), vmem(c_half, width),
            vmem(others, c_half // z_devices, width), vmem(c_half // z_devices, width), vmem(width, width),
            dma, dma((2,)), dma((2,)), dma, dma,
            dma((others,)), dma((others,)), dma((others,)), dma((others,)), dma((4, z_devices)), dma((2,)),
            dma, dma, dma((others,)), dma((others,)), dma((others,)), dma, dma, dma,
        ],
        compiler_params=pltpu.CompilerParams(
            collective_id=0, has_side_effects=True, vmem_limit_bytes=32 * 1024 * 1024
        ),
        cost_estimate=pl.CostEstimate(
            flops=40 * 3 * 2 * width**3, bytes_accessed=8 * rows * width, transcendentals=4096
        ),
        name="rotate_pairs",
    )(pltpu.with_memory_space_constraint(x, pltpu.MemorySpace.HBM))


def solution(mesh):
    run = functools.partial(shards, mesh.shape["blk"], mesh.shape["row"] // 2)
    return jax.shard_map(
        run, mesh=mesh, in_specs=(P("row", "blk"),), out_specs=P("row", "blk"), check_vma=False
    )
```

time: 283 us -> 42.6 us (0.15)
  the two profiles are of different devices: /device:TPU:1 before, /device:TPU:49 now
where the time goes in v2:
time: 42.6 us; the launch traced here: 42.4 us
  Pallas kernels  41.7 us (98%)
  local copies, waits for them, and re-layouts  0.71 us (2%)
    pallas_call x1, Pallas kernels, shards(): pl.pallas_call(functools.partial(kernel, blk_devices, z_devices), out_sha...  41.7 us

profile of v2, /device:TPU:49, one launch (start us, length us, event | category | flops | bytes accessed | tf_op | source)
XLA Modules:
  0.0 42.4 jit_solution(3346683859818849496)
XLA Ops:
  0.0 41.7 %rotate_pairs.1 = f32[256,256]{1,0:T(8,128)S(1)} custom-call(f32[256,256]{1,0:T(8,128)} %x_hbm.1), custom_call_target="tpu_custom_call" | custom-call | flops 4026531840 | bytes 524288 | tf_op jit(solution)/shard_map/rotate_pairs/pallas_call | solution.py:300
  41.7 0.7 %copy.3 = f32[256,256]{1,0:T(8,128)} copy(f32[256,256]{1,0:T(8,128)S(1)} %rotate_pairs.1) | data formatting | bytes 524288

commit v3 on v2

v3 whole, which is shorter than its diff:
```python
import functools
import math

import jax
import jax.numpy as jnp
from jax import lax
from jax.experimental import pallas as pl
from jax.experimental.pallas import tpu as pltpu
from jax.sharding import PartitionSpec as P

NSTEPS = 5
MESH = pl.DeviceIdType.MESH


def product(a, b, lhs_dim=1):
    return lax.dot_general(
        a, b, (((lhs_dim,), (0,)), ((), ())), preferred_element_type=jnp.float32
    )


def split(a):
    high = a.astype(jnp.bfloat16)
    return high, (a - high.astype(jnp.float32)).astype(jnp.bfloat16)


def dot3(a, b, lhs_dim=1):
    high, low = a
    if lhs_dim == 0:
        return product(high, b[0], 0) + (product(high, b[1], 0) + product(low, b[0], 0))
    half = high.shape[0] // 2
    blocks = []
    for rows in (slice(0, half), slice(half, 2 * half)):
        small = product(high[rows], b[1]) + product(low[rows], b[0])
        blocks.append(product(high[rows], b[0]) + small)
    return jnp.concatenate(blocks, axis=0)


def eye(n):
    rows = lax.broadcasted_iota(jnp.int32, (n, n), 0)
    columns = lax.broadcasted_iota(jnp.int32, (n, n), 1)
    return rows == columns


def diagonals(a):
    kept = jnp.where(eye(a.shape[0]), a, 0.0)
    return jnp.sum(kept, axis=1, keepdims=True), jnp.sum(kept, axis=0, keepdims=True)


class Solve:
    def __init__(self, starts):
        self.eye = jnp.where(eye(starts[0].shape[0]), 1.5, 0.0)
        y = [0.25 * m for m in starts]
        self.z = [self.eye - m for m in y]
        self.f = self.z_split = [split(z) for z in self.z]
        self.y = [dot3(f, split(m)) for f, m in zip(self.f, y)]
        self.y_split = [split(m) for m in self.y]

    def factors(self):
        self.f = [split(self.eye - dot3(y, z)) for y, z in zip(self.y_split, self.z_split)]

    def step(self):
        self.factors()
        self.z = [dot3(f, z) for f, z in zip(self.f, self.z_split)]
        self.z_split = [split(z) for z in self.z]
        self.y = [dot3(f, y) for f, y in zip(self.f, self.y_split)]
        self.y_split = [split(y) for y in self.y]


def half_of(a, second, axis):
    n = a.shape[axis] // 2
    first = lax.slice_in_dim(a, 0, n, axis=axis)
    return jnp.where(second, lax.slice_in_dim(a, n, 2 * n, axis=axis), first)


def kernel(
    blk_devices, z_devices,
    x_hbm, out_ref,
    x_ref, moved, gram_local, gram_core, gram_sum, gram_parts, gram_full, grams,
    cross_local, cross_core, cross_sum, cross_parts, cross_shard, cross,
    here_sem, load_sem, x_send, x_recv, gc_send, gc_recv, gz_send, gz_recv, ga_send, ga_recv,
    straight_send, across_send, gx_recv, cc_send, cc_recv, cz_send, cz_recv, ca_send, ca_recv, cf_send, cf_recv,
):
    k = lax.axis_index("blk")
    row = lax.axis_index("row")
    z = row // 2
    core = row % 2
    is_first = k == 0
    is_last = k == blk_devices - 1
    up = jnp.minimum(k + 1, blk_devices - 1)
    down = jnp.maximum(k - 1, 0)
    up_slot = jnp.where(is_last, 1, 0)
    down_slot = jnp.where(is_first, 0, 1)
    second = (k == 1, jnp.logical_not(is_last))
    half_width = x_ref.shape[1] // 2
    g_half = gram_local.shape[0] // 2
    g_part = g_half // z_devices
    c_half = cross_local.shape[0] // 2
    c_part = c_half // z_devices
    z_half_devices = z_devices // 2
    z_side = z // z_half_devices
    far_first = sorted(range(1, z_devices), key=lambda t: -min(t, z_devices - t))

    def peer(blk, t, other=False):
        return {"blk": blk, "row": lax.rem(z + t, z_devices) * 2 + (1 - core if other else core)}

    sibling = peer(k, 0, True)

    def remote(src, dst, send, recv, device):
        return pltpu.make_async_remote_copy(
            src_ref=src, dst_ref=dst, send_sem=send, recv_sem=recv,
            device_id=device, device_id_type=MESH,
        )

    def wait_for(ref, sem):
        pltpu.make_async_copy(ref, ref, sem).wait()

    def rows_at(start, size):
        return pl.ds(pl.multiple_of(start, 8), size)

    def either(condition, yes, no):
        pl.when(condition)(lambda: yes() and None)
        pl.when(jnp.logical_not(condition))(lambda: no() and None)

    def signal(sem, device):
        pl.semaphore_signal(sem, inc=1, device_id=device, device_id_type=MESH)

    load = pltpu.make_async_copy(x_hbm, x_ref, load_sem)
    load.start()

    barrier = pltpu.get_barrier_semaphore()
    for t in range(z_devices - 1, 0, -1):
        pl.when(z + t < z_devices)(functools.partial(signal, barrier, peer(k, t)))
    for edge, blk in ((is_last, up), (is_first, down)):
        for other in (False, True):
            pl.when(jnp.logical_not(edge))(functools.partial(signal, barrier, peer(blk, 0, other)))
    signal(barrier, sibling)

    load.wait()
    x_split = split(x_ref[...])
    g = dot3(x_split, x_split, 0)
    gram_local[:half_width] = g[:half_width, :half_width]
    gram_local[half_width : 2 * half_width] = g[:half_width, half_width:]
    gram_local[2 * half_width :] = g[half_width:, half_width:]

    neighbours = 2 - is_first.astype(jnp.int32) - is_last.astype(jnp.int32)
    pl.semaphore_wait(barrier, z + 1 + 2 * neighbours)
    for t in range(z_devices - 1, 0, -1):
        pl.when(z - t >= 0)(functools.partial(signal, here_sem, peer(k, z_devices - t)))

    gc = remote(gram_local.at[rows_at((1 - core) * g_half, g_half)], gram_core, gc_send, gc_recv, sibling)
    gc.start()

    x_up = remote(x_ref, moved.at[up_slot], x_send.at[0], x_recv.at[up_slot], peer(up, 0))
    x_down = remote(x_ref, moved.at[down_slot], x_send.at[1], x_recv.at[down_slot], peer(down, 0))
    either(is_last, pltpu.make_async_copy(x_ref, moved.at[1], x_recv.at[1]).start, x_up.start)
    either(is_first, pltpu.make_async_copy(x_ref, moved.at[0], x_recv.at[0]).start, x_down.start)

    def scatter(total, part, parts, send, recv):
        for t in far_first:
            there = rows_at(lax.rem(z + t, z_devices) * part, part)
            remote(total.at[there], parts.at[t - 1], send, recv, peer(k, t)).start()

    def gather(total, part, parts, recv):
        wait_for(parts, recv)
        terms = [total[rows_at(z * part, part)]] + [parts[n] for n in range(z_devices - 1)]
        while len(terms) > 1:
            terms = [a + b for a, b in zip(terms[::2], terms[1::2])]
        return terms[0]

    gc.wait_recv()
    gram_sum[...] = gram_local[rows_at(core * g_half, g_half)] + gram_core[...]

    @pl.when(z < z_devices - 1)
    def _():
        pl.semaphore_wait(here_sem, z_devices - 1 - z)

    scatter(gram_sum, g_part, gram_parts, gz_send, gz_recv)
    own_rows = rows_at(z * g_part, g_part)
    gram_full[own_rows] = gather(gram_sum, g_part, gram_parts, gz_recv)
    for t in far_first:
        remote(gram_full.at[own_rows], gram_full.at[own_rows], ga_send, ga_recv.at[z_side], peer(k, t)).start()

    for slot in range(2):
        wait_for(moved.at[slot], x_recv.at[slot])
    moved_split = [split(moved[slot]) for slot in range(2)]
    cross_local[...] = dot3(*moved_split, 0)
    cc = remote(cross_local.at[rows_at((1 - core) * c_half, c_half)], cross_core, cc_send, cc_recv, sibling)
    cc.start()
    cc.wait_recv()
    cross_sum[...] = cross_local[rows_at(core * c_half, c_half)] + cross_core[...]
    scatter(cross_sum, c_part, cross_parts, cz_send, cz_recv)

    side_rows = z_half_devices * g_part
    for side, count in ((z_side, z_half_devices - 1), (1 - z_side, z_half_devices)):
        wait_for(gram_full.at[pl.ds(0, count * g_part)], ga_recv.at[side])
        src = gram_full.at[rows_at(side * side_rows, side_rows)]
        there = rows_at(core * g_half + side * side_rows, side_rows)
        for n, (edge, blk, slot, own_slot) in enumerate(((is_last, up, up_slot, 1), (is_first, down, down_slot, 0))):
            dst = grams.at[slot, there]
            straight = remote(src, dst, straight_send.at[n], gx_recv.at[slot], peer(blk, 0))
            stays = pltpu.make_async_copy(src, grams.at[own_slot, there], gx_recv.at[own_slot])
            either(edge, stays.start, straight.start)
            remote(src, dst, across_send, gx_recv.at[slot], peer(blk, 0, True)).start()

    cross_shard[...] = gather(cross_sum, c_part, cross_parts, cz_recv)
    c_mine = rows_at(core * c_half + z * c_part, c_part)
    for t in far_first:
        remote(cross_shard, cross.at[c_mine], ca_send, ca_recv, peer(k, t)).start()
    pltpu.make_async_copy(cross_shard, cross.at[c_mine], ca_recv).start()

    for slot in range(2):
        wait_for(grams.at[slot], gx_recv.at[slot])
    diag_rows, roots_columns, scaled = [], [], []
    for slot in range(2):
        g = grams[slot]
        upper = g[half_width : 2 * half_width]
        full = jnp.concatenate(
            [
                jnp.concatenate([g[:half_width], upper], axis=1),
                jnp.concatenate([upper.T, g[2 * half_width :]], axis=1),
            ],
            axis=0,
        )
        column, line = diagonals(full)
        diag_rows.append(line)
        roots_columns.append(lax.rsqrt(column))
        scaled.append(full * roots_columns[slot] * lax.rsqrt(line))
    first = Solve(scaled)
    for _ in range(NSTEPS - 2):
        first.step()
    first.factors()
    zs, t_rows, its, ul = [], [], [], []
    for n in range(2):
        z_half = dot3(first.f[n], split(half_of(first.z[n], second[n], 1)))
        y_half = dot3(first.f[n], split(half_of(first.y[n], second[n], 1)))
        own = 4.0 * dot3(split(z_half), split(y_half), 0)
        t_column, t_row = diagonals(own)
        it_row = lax.rsqrt(t_row)
        t_rows.append(t_row)
        z_unit = z_half * it_row
        zs.append(split(z_unit))
        its.append(own * lax.rsqrt(t_column) * it_row)
        ul.append(split(dot3(moved_split[n], split(z_unit * roots_columns[n]))))
    ul = [jnp.concatenate([ul[0][p], ul[1][p]], axis=1) for p in range(2)]
    diag2 = jnp.concatenate([half_of(diag_rows[n], second[n], 1) * t_rows[n] for n in range(2)], axis=1)
    ends = math.sqrt(0.5) * jnp.sqrt(0.5 * diag2)
    root_row = lax.rsqrt(diag_rows[1])

    gc.wait_send()
    cc.wait_send()
    for parts, sem in ((gram_parts, gz_send), (gram_parts, ga_send), (cross_parts, cz_send), (cross_parts, ca_send)):
        wait_for(parts, sem)
    wait_for(grams.at[0], across_send)
    for n, (edge, copy) in enumerate(((is_last, x_up), (is_first, x_down))):

        @pl.when(jnp.logical_not(edge))
        def _(n=n, copy=copy):
            copy.wait_send()
            wait_for(gram_full, straight_send.at[n])

    here = cross.at[rows_at(core * c_half, c_half)]
    wait_for(here, ca_recv)
    cf = remote(here, here, cf_send, cf_recv, sibling)
    cf.start()
    cf.wait_recv()

    cross_scaled = cross[...] * roots_columns[0] * root_row
    off = dot3(zs[0], split(dot3(split(cross_scaled), zs[1])), 0)
    scaled2 = jnp.concatenate(
        [jnp.concatenate([its[0], off], axis=1), jnp.concatenate([off.T, its[1]], axis=1)], axis=0
    )
    last = Solve([scaled2])
    for _ in range(NSTEPS - 2):
        last.step()
    last.factors()
    almost = dot3(ul, last.z_split[0])
    out_ref[...] = dot3(split(almost), last.f[0]) * ends
    cf.wait_send()


def shards(blk_devices, z_devices, x):
    rows, width = x.shape
    half = width // 2
    dma = pltpu.SemaphoreType.DMA
    g_half, c_half = 3 * half // 2, width // 2
    others = z_devices - 1
    vmem = lambda *shape: pltpu.VMEM(shape, jnp.float32)
    return pl.pallas_call(
        functools.partial(kernel, blk_devices, z_devices),
        out_shape=jax.ShapeDtypeStruct(x.shape, jnp.float32),
        in_specs=[pl.BlockSpec(memory_space=pltpu.MemorySpace.HBM)],
        out_specs=pl.BlockSpec(memory_space=pltpu.VMEM),
        scratch_shapes=[
            vmem(rows, width), vmem(2, rows, width),
            vmem(3 * half, half), vmem(g_half, half), vmem(g_half, half),
            vmem(others, g_half // z_devices, half), vmem(g_half, half), vmem(2, 3 * half, half),
            vmem(width, width), vmem(c_half, width), vmem(c_half, width),
            vmem(others, c_half // z_devices, width), vmem(c_half // z_devices, width), vmem(width, width),
            pltpu.SemaphoreType.REGULAR, dma, dma((2,)), dma((2,)), dma, dma, dma, dma, dma, dma((2,)),
            dma((2,)), dma, dma((2,)), dma, dma, dma, dma, dma, dma, dma, dma,
        ],
        compiler_params=pltpu.CompilerParams(
            collective_id=0, has_side_effects=True, vmem_limit_bytes=32 * 1024 * 1024
        ),
        cost_estimate=pl.CostEstimate(
            flops=40 * 3 * 2 * width**3, bytes_accessed=8 * rows * width, transcendentals=4096
        ),
        name="rotate_pairs",
    )(pltpu.with_memory_space_constraint(x, pltpu.MemorySpace.HBM))


def solution(mesh):
    run = functools.partial(shards, mesh.shape["blk"], mesh.shape["row"] // 2)
    return jax.shard_map(
        run, mesh=mesh, in_specs=(P("row", "blk"),), out_specs=P("row", "blk"), check_vma=False
    )
```

time: 42.6 us -> 37.5 us (0.88)
  the two profiles are of different devices: /device:TPU:49 before, /device:TPU:33 now
where the time goes in v3:
time: 37.5 us; the launch traced here: 37.4 us
  Pallas kernels  36.7 us (98%)
  local copies, waits for them, and re-layouts  0.71 us (2%)
    pallas_call x1, Pallas kernels, shards(): pl.pallas_call(functools.partial(kernel, blk_devices, z_devices), out_sha...  36.7 us

profile of v3, /device:TPU:33, one launch (start us, length us, event | category | flops | bytes accessed | tf_op | source)
XLA Modules:
  0.0 37.4 jit_solution(12209472920630575204)
XLA Ops:
  0.0 36.7 %rotate_pairs.1 = f32[256,256]{1,0:T(8,128)S(1)} custom-call(f32[256,256]{1,0:T(8,128)} %x_hbm.1), custom_call_target="tpu_custom_call" | custom-call | flops 4026531840 | bytes 524288 | tf_op jit(solution)/shard_map/rotate_pairs/pallas_call | solution.py:288
  36.7 0.7 %copy.3 = f32[256,256]{1,0:T(8,128)} copy(f32[256,256]{1,0:T(8,128)S(1)} %rotate_pairs.1) | data formatting | bytes 524288

commit v4 on v3

--- a/solution.py
+++ b/solution.py
@@ -76,7 +76,7 @@
     blk_devices, z_devices,
     x_hbm, out_ref,
     x_ref, moved, gram_local, gram_core, gram_sum, gram_parts, gram_full, grams,
-    cross_local, cross_core, cross_sum, cross_parts, cross_shard, cross,
+    cross_local, cross_core, cross_sum, cross_parts, cross_shard, cross, mixed_local, mixed_core,
     here_sem, load_sem, x_send, x_recv, gc_send, gc_recv, gz_send, gz_recv, ga_send, ga_recv,
     straight_send, across_send, gx_recv, cc_send, cc_recv, cz_send, cz_recv, ca_send, ca_recv, cf_send, cf_recv,
 ):
@@ -94,7 +94,7 @@
     half_width = x_ref.shape[1] // 2
     g_half = gram_local.shape[0] // 2
     g_part = g_half // z_devices
-    c_half = cross_local.shape[0] // 2
+    c_half = cross_local.shape[0]
     c_part = c_half // z_devices
     z_half_devices = z_devices // 2
     z_side = z // z_half_devices
@@ -128,37 +128,37 @@
     load.start()
 
     barrier = pltpu.get_barrier_semaphore()
-    for t in range(z_devices - 1, 0, -1):
-        pl.when(z + t < z_devices)(functools.partial(signal, barrier, peer(k, t)))
     for edge, blk in ((is_last, up), (is_first, down)):
         for other in (False, True):
             pl.when(jnp.logical_not(edge))(functools.partial(signal, barrier, peer(blk, 0, other)))
     signal(barrier, sibling)
-
+    for t in range(z_devices - 1, 0, -1):
+        pl.when(z + t < z_devices)(functools.partial(signal, barrier, peer(k, t)))
+    neighbours = 2 - is_first.astype(jnp.int32) - is_last.astype(jnp.int32)
     load.wait()
+    pl.semaphore_wait(barrier, z + 1 + 2 * neighbours)
+
+    x_up = remote(x_ref, moved.at[up_slot], x_send.at[0], x_recv.at[up_slot], peer(up, 0))
+    x_down = remote(x_ref, moved.at[down_slot], x_send.at[1], x_recv.at[down_slot], peer(down, 0))
+    either(is_last, pltpu.make_async_copy(x_ref, moved.at[1], x_recv.at[1]).start, x_up.start)
+    either(is_first, pltpu.make_async_copy(x_ref, moved.at[0], x_recv.at[0]).start, x_down.start)
+
+    for t in range(z_devices - 1, 0, -1):
+        pl.when(z - t >= 0)(functools.partial(signal, here_sem.at[t - 1], peer(k, z_devices - t)))
+
     x_split = split(x_ref[...])
     g = dot3(x_split, x_split, 0)
     gram_local[:half_width] = g[:half_width, :half_width]
     gram_local[half_width : 2 * half_width] = g[:half_width, half_width:]
     gram_local[2 * half_width :] = g[half_width:, half_width:]
 
-    neighbours = 2 - is_first.astype(jnp.int32) - is_last.astype(jnp.int32)
-    pl.semaphore_wait(barrier, z + 1 + 2 * neighbours)
-    for t in range(z_devices - 1, 0, -1):
-        pl.when(z - t >= 0)(functools.partial(signal, here_sem, peer(k, z_devices - t)))
-
     gc = remote(gram_local.at[rows_at((1 - core) * g_half, g_half)], gram_core, gc_send, gc_recv, sibling)
     gc.start()
 
-    x_up = remote(x_ref, moved.at[up_slot], x_send.at[0], x_recv.at[up_slot], peer(up, 0))
-    x_down = remote(x_ref, moved.at[down_slot], x_send.at[1], x_recv.at[down_slot], peer(down, 0))
-    either(is_last, pltpu.make_async_copy(x_ref, moved.at[1], x_recv.at[1]).start, x_up.start)
-    either(is_first, pltpu.make_async_copy(x_ref, moved.at[0], x_recv.at[0]).start, x_down.start)
-
-    def scatter(total, part, parts, send, recv):
-        for t in far_first:
-            there = rows_at(lax.rem(z + t, z_devices) * part, part)
-            remote(total.at[there], parts.at[t - 1], send, recv, peer(k, t)).start()
+    def to_others(src, dst, send, recv):
+        for there in range(z_devices):
+            copy = remote(src, dst, send, recv, {"blk": k, "row": there * 2 + core})
+            pl.when(z != there)(copy.start)
 
     def gather(total, part, parts, recv):
         wait_for(parts, recv)
@@ -169,26 +169,37 @@
 
     gc.wait_recv()
     gram_sum[...] = gram_local[rows_at(core * g_half, g_half)] + gram_core[...]
-
-    @pl.when(z < z_devices - 1)
-    def _():
-        pl.semaphore_wait(here_sem, z_devices - 1 - z)
-
-    scatter(gram_sum, g_part, gram_parts, gz_send, gz_recv)
+    for owner in sorted(range(z_devices), key=lambda n: -min(n, z_devices - n)):
+
+        @pl.when(z < owner)
+        def _(owner=owner):
+            pl.semaphore_wait(here_sem.at[owner - z - 1], 1)
+
+        t = lax.rem(owner - z + z_devices, z_devices)
+        copy = remote(
+            gram_sum.at[pl.ds(owner * g_part, g_part)], gram_parts.at[t - 1], gz_send, gz_recv,
+            {"blk": k, "row": owner * 2 + core},
+        )
+        pl.when(z != owner)(copy.start)
+
     own_rows = rows_at(z * g_part, g_part)
+
     gram_full[own_rows] = gather(gram_sum, g_part, gram_parts, gz_recv)
-    for t in far_first:
-        remote(gram_full.at[own_rows], gram_full.at[own_rows], ga_send, ga_recv.at[z_side], peer(k, t)).start()
+    to_others(gram_full.at[own_rows], gram_full.at[own_rows], ga_send, ga_recv.at[z_side])
 
     for slot in range(2):
         wait_for(moved.at[slot], x_recv.at[slot])
-    moved_split = [split(moved[slot]) for slot in range(2)]
-    cross_local[...] = dot3(*moved_split, 0)
-    cc = remote(cross_local.at[rows_at((1 - core) * c_half, c_half)], cross_core, cc_send, cc_recv, sibling)
+    b_split = split(moved[1])
+    a_half = [half_of(moved[0], core == which, 1) for which in (0, 1)]
+    cross_local[...] = dot3(split(a_half[0]), b_split, 0)
+    cc = remote(cross_local, cross_core, cc_send, cc_recv, sibling)
     cc.start()
+    cross_sum[...] = dot3(split(a_half[1]), b_split, 0)
     cc.wait_recv()
-    cross_sum[...] = cross_local[rows_at(core * c_half, c_half)] + cross_core[...]
-    scatter(cross_sum, c_part, cross_parts, cz_send, cz_recv)
+    cross_sum[...] += cross_core[...]
+    for t in far_first:
+        there = rows_at(lax.rem(z + t, z_devices) * c_part, c_part)
+        remote(cross_sum.at[there], cross_parts.at[t - 1], cz_send, cz_recv, peer(k, t)).start()
 
     side_rows = z_half_devices * g_part
     for side, count in ((z_side, z_half_devices - 1), (1 - z_side, z_half_devices)):
@@ -203,9 +214,8 @@
             remote(src, dst, across_send, gx_recv.at[slot], peer(blk, 0, True)).start()
 
     cross_shard[...] = gather(cross_sum, c_part, cross_parts, cz_recv)
-    c_mine = rows_at(core * c_half + z * c_part, c_part)
-    for t in far_first:
-        remote(cross_shard, cross.at[c_mine], ca_send, ca_recv, peer(k, t)).start()
+    c_mine = rows_at(z * c_part, c_part)
+    to_others(cross_shard, cross.at[c_mine], ca_send, ca_recv)
     pltpu.make_async_copy(cross_shard, cross.at[c_mine], ca_recv).start()
 
     for slot in range(2):
@@ -230,6 +240,7 @@
         first.step()
     first.factors()
     zs, t_rows, its, ul = [], [], [], []
+    moved_split = [split(moved[slot]) for slot in range(2)]
     for n in range(2):
         z_half = dot3(first.f[n], split(half_of(first.z[n], second[n], 1)))
         y_half = dot3(first.f[n], split(half_of(first.y[n], second[n], 1)))
@@ -238,10 +249,9 @@
         it_row = lax.rsqrt(t_row)
         t_rows.append(t_row)
         z_unit = z_half * it_row
-        zs.append(split(z_unit))
+        zs.append(z_unit)
         its.append(own * lax.rsqrt(t_column) * it_row)
-        ul.append(split(dot3(moved_split[n], split(z_unit * roots_columns[n]))))
-    ul = [jnp.concatenate([ul[0][p], ul[1][p]], axis=1) for p in range(2)]
+        ul.append(split(z_unit * roots_columns[n]))
     diag2 = jnp.concatenate([half_of(diag_rows[n], second[n], 1) * t_rows[n] for n in range(2)], axis=1)
     ends = math.sqrt(0.5) * jnp.sqrt(0.5 * diag2)
     root_row = lax.rsqrt(diag_rows[1])
@@ -258,19 +268,24 @@
             copy.wait_send()
             wait_for(gram_full, straight_send.at[n])
 
-    here = cross.at[rows_at(core * c_half, c_half)]
-    wait_for(here, ca_recv)
-    cf = remote(here, here, cf_send, cf_recv, sibling)
+    z_rows = split(half_of(zs[0], core == 1, 0))
+    z_other = split(zs[1])
+    roots_half = half_of(roots_columns[0], core == 1, 0)
+    wait_for(cross, ca_recv)
+    turned = dot3(split(cross[...] * roots_half * root_row), z_other)
+    mixed_local[...] = dot3(z_rows, split(turned), 0)
+    cf = remote(mixed_local, mixed_core, cf_send, cf_recv, sibling)
     cf.start()
     cf.wait_recv()
-
-    cross_scaled = cross[...] * roots_columns[0] * root_row
-    off = dot3(zs[0], split(dot3(split(cross_scaled), zs[1])), 0)
+    off = mixed_local[...] + mixed_core[...]
     scaled2 = jnp.concatenate(
         [jnp.concatenate([its[0], off], axis=1), jnp.concatenate([off.T, its[1]], axis=1)], axis=0
     )
     last = Solve([scaled2])
-    for _ in range(NSTEPS - 2):
+    last.step()
+    ul = [split(dot3(moved_split[n], ul[n])) for n in range(2)]
+    ul = [jnp.concatenate([ul[0][p], ul[1][p]], axis=1) for p in range(2)]
+    for _ in range(NSTEPS - 3):
         last.step()
     last.factors()
     almost = dot3(ul, last.z_split[0])
@@ -294,9 +309,10 @@
             vmem(rows, width), vmem(2, rows, width),
             vmem(3 * half, half), vmem(g_half, half), vmem(g_half, half),
             vmem(others, g_half // z_devices, half), vmem(g_half, half), vmem(2, 3 * half, half),
-            vmem(width, width), vmem(c_half, width), vmem(c_half, width),
-            vmem(others, c_half // z_devices, width), vmem(c_half // z_devices, width), vmem(width, width),
-            pltpu.SemaphoreType.REGULAR, dma, dma((2,)), dma((2,)), dma, dma, dma, dma, dma, dma((2,)),
+            vmem(c_half, width), vmem(c_half, width), vmem(c_half, width),
+            vmem(others, c_half // z_devices, width), vmem(c_half // z_devices, width), vmem(c_half, width),
+            vmem(half, half), vmem(half, half),
+            pltpu.SemaphoreType.REGULAR((others,)), dma, dma((2,)), dma((2,)), dma, dma, dma, dma, dma, dma((2,)),
             dma((2,)), dma, dma((2,)), dma, dma, dma, dma, dma, dma, dma, dma,
         ],
         compiler_params=pltpu.CompilerParams(

time: 37.5 us -> 36.3 us (0.968)
  the two profiles are of different devices: /device:TPU:33 before, /device:TPU:49 now
where the time goes in v4:
time: 36.3 us; the launch traced here: 36.2 us
  Pallas kernels  35.4 us (98%)
  local copies, waits for them, and re-layouts  0.71 us (2%)
    pallas_call x1, Pallas kernels, shards(): pl.pallas_call(functools.partial(kernel, blk_devices, z_devices), out_sha...  35.4 us

profile of v4, /device:TPU:49, one launch (start us, length us, event | category | flops | bytes accessed | tf_op | source)
XLA Modules:
  0.0 36.2 jit_solution(9053531908091014745)
XLA Ops:
  0.0 35.4 %rotate_pairs.1 = f32[256,256]{1,0:T(8,128)S(1)} custom-call(f32[256,256]{1,0:T(8,128)} %x_hbm.1), custom_call_target="tpu_custom_call" | custom-call | flops 4026531840 | bytes 524288 | tf_op jit(solution)/shard_map/rotate_pairs/pallas_call | solution.py:303
  35.5 0.7 %copy.3 = f32[256,256]{1,0:T(8,128)} copy(f32[256,256]{1,0:T(8,128)S(1)} %rotate_pairs.1) | data formatting | bytes 524288

commit v5 on v4

--- a/solution.py
+++ b/solution.py
@@ -75,7 +75,7 @@
 def kernel(
     blk_devices, z_devices,
     x_hbm, out_ref,
-    x_ref, moved, gram_local, gram_core, gram_sum, gram_parts, gram_full, grams,
+    x_ref, moved, gram_local, gram_core, gram_sum, gram_parts, gram_shard, gram_full, grams,
     cross_local, cross_core, cross_sum, cross_parts, cross_shard, cross, mixed_local, mixed_core,
     here_sem, load_sem, x_send, x_recv, gc_send, gc_recv, gz_send, gz_recv, ga_send, ga_recv,
     straight_send, across_send, gx_recv, cc_send, cc_recv, cz_send, cz_recv, ca_send, ca_recv, cf_send, cf_recv,
@@ -93,11 +93,12 @@
     second = (k == 1, jnp.logical_not(is_last))
     half_width = x_ref.shape[1] // 2
     g_half = gram_local.shape[0] // 2
-    g_part = g_half // z_devices
+    g_part = half_width // z_devices
+    g_parts = [(0, g_part + 8)] + [(8 + n * g_part, g_part) for n in range(1, z_devices)]
     c_half = cross_local.shape[0]
     c_part = c_half // z_devices
-    z_half_devices = z_devices // 2
-    z_side = z // z_half_devices
+    middle = z_devices // 2
+    lower_side = z < middle
     far_first = sorted(range(1, z_devices), key=lambda t: -min(t, z_devices - t))
 
     def peer(blk, t, other=False):
@@ -148,9 +149,14 @@
 
     x_split = split(x_ref[...])
     g = dot3(x_split, x_split, 0)
-    gram_local[:half_width] = g[:half_width, :half_width]
-    gram_local[half_width : 2 * half_width] = g[:half_width, half_width:]
-    gram_local[2 * half_width :] = g[half_width:, half_width:]
+    block_rows = lax.broadcasted_iota(jnp.int32, (half_width, half_width), 0)
+    block_columns = lax.broadcasted_iota(jnp.int32, (half_width, half_width), 1)
+    gram_local[:half_width] = g[:half_width, half_width:]
+    gram_local[half_width:g_half] = jnp.zeros((8, half_width), jnp.float32)
+    gram_local[g_half : g_half + half_width] = jnp.where(
+        block_rows >= block_columns, g[:half_width, :half_width], g[half_width:, half_width:]
+    )
+    gram_local[g_half + half_width :] = jnp.broadcast_to(diagonals(g[half_width:, half_width:])[1], (8, half_width))
 
     gc = remote(gram_local.at[rows_at((1 - core) * g_half, g_half)], gram_core, gc_send, gc_recv, sibling)
     gc.start()
@@ -160,9 +166,7 @@
             copy = remote(src, dst, send, recv, {"blk": k, "row": there * 2 + core})
             pl.when(z != there)(copy.start)
 
-    def gather(total, part, parts, recv):
-        wait_for(parts, recv)
-        terms = [total[rows_at(z * part, part)]] + [parts[n] for n in range(z_devices - 1)]
+    def tree(terms):
         while len(terms) > 1:
             terms = [a + b for a, b in zip(terms[::2], terms[1::2])]
         return terms[0]
@@ -176,16 +180,28 @@
             pl.semaphore_wait(here_sem.at[owner - z - 1], 1)
 
         t = lax.rem(owner - z + z_devices, z_devices)
+        start, size = g_parts[owner]
         copy = remote(
-            gram_sum.at[pl.ds(owner * g_part, g_part)], gram_parts.at[t - 1], gz_send, gz_recv,
+            gram_sum.at[pl.ds(start, size)], gram_parts.at[jnp.maximum(t - 1, 0), pl.ds(0, size)], gz_send, gz_recv,
             {"blk": k, "row": owner * 2 + core},
         )
         pl.when(z != owner)(copy.start)
 
-    own_rows = rows_at(z * g_part, g_part)
-
-    gram_full[own_rows] = gather(gram_sum, g_part, gram_parts, gz_recv)
-    to_others(gram_full.at[own_rows], gram_full.at[own_rows], ga_send, ga_recv.at[z_side])
+    def own_part(start, size):
+        wait_for(grams.at[0, pl.ds(0, (z_devices - 1) * size)], gz_recv)
+        gram_shard[:size] = tree(
+            [gram_sum[pl.ds(start, size)]] + [gram_parts[n, :size] for n in range(z_devices - 1)]
+        )
+        src, dst = gram_shard.at[pl.ds(0, size)], gram_full.at[pl.ds(start, size)]
+        sem = ga_recv.at[jnp.where(lower_side, 0, 1)]
+        pltpu.make_async_copy(src, dst, sem).start()
+        to_others(src, dst, ga_send, sem)
+
+    either(
+        z == 0,
+        functools.partial(own_part, *g_parts[0]),
+        lambda: own_part(pl.multiple_of(8 + z * g_part, 8), g_part),
+    )
 
     for slot in range(2):
         wait_for(moved.at[slot], x_recv.at[slot])
@@ -201,11 +217,12 @@
         there = rows_at(lax.rem(z + t, z_devices) * c_part, c_part)
         remote(cross_sum.at[there], cross_parts.at[t - 1], cz_send, cz_recv, peer(k, t)).start()
 
-    side_rows = z_half_devices * g_part
-    for side, count in ((z_side, z_half_devices - 1), (1 - z_side, z_half_devices)):
-        wait_for(gram_full.at[pl.ds(0, count * g_part)], ga_recv.at[side])
-        src = gram_full.at[rows_at(side * side_rows, side_rows)]
-        there = rows_at(core * g_half + side * side_rows, side_rows)
+    def forward(side):
+        start = g_parts[side * middle][0]
+        size = (g_parts[middle][0], g_half - g_parts[middle][0])[side]
+        src = gram_full.at[pl.ds(start, size)]
+        there = rows_at(core * g_half + start, size)
+        wait_for(src, ga_recv.at[side])
         for n, (edge, blk, slot, own_slot) in enumerate(((is_last, up, up_slot, 1), (is_first, down, down_slot, 0))):
             dst = grams.at[slot, there]
             straight = remote(src, dst, straight_send.at[n], gx_recv.at[slot], peer(blk, 0))
@@ -213,7 +230,10 @@
             either(edge, stays.start, straight.start)
             remote(src, dst, across_send, gx_recv.at[slot], peer(blk, 0, True)).start()
 
-    cross_shard[...] = gather(cross_sum, c_part, cross_parts, cz_recv)
+    either(lower_side, lambda: (forward(0), forward(1)), lambda: (forward(1), forward(0)))
+
+    wait_for(cross_parts, cz_recv)
+    cross_shard[...] = tree([cross_sum[rows_at(z * c_part, c_part)]] + [cross_parts[n] for n in range(z_devices - 1)])
     c_mine = rows_at(z * c_part, c_part)
     to_others(cross_shard, cross.at[c_mine], ca_send, ca_recv)
     pltpu.make_async_copy(cross_shard, cross.at[c_mine], ca_recv).start()
@@ -222,12 +242,14 @@
         wait_for(grams.at[slot], gx_recv.at[slot])
     diag_rows, roots_columns, scaled = [], [], []
     for slot in range(2):
-        g = grams[slot]
-        upper = g[half_width : 2 * half_width]
+        upper = grams[slot, pl.ds(0, half_width)]
+        packed = grams[slot, pl.ds(g_half, half_width)]
+        corner = jnp.where(block_rows < block_columns, packed, packed.T)
+        corner = jnp.where(block_rows == block_columns, grams[slot, pl.ds(g_half + half_width, 1)], corner)
         full = jnp.concatenate(
             [
-                jnp.concatenate([g[:half_width], upper], axis=1),
-                jnp.concatenate([upper.T, g[2 * half_width :]], axis=1),
+                jnp.concatenate([jnp.where(block_rows >= block_columns, packed, packed.T), upper], axis=1),
+                jnp.concatenate([upper.T, corner], axis=1),
             ],
             axis=0,
         )
@@ -258,8 +280,19 @@
 
     gc.wait_send()
     cc.wait_send()
-    for parts, sem in ((gram_parts, gz_send), (gram_parts, ga_send), (cross_parts, cz_send), (cross_parts, ca_send)):
-        wait_for(parts, sem)
+    wait_for(cross_parts, cz_send)
+    wait_for(cross_parts, ca_send)
+
+    def own_sent(gz_rows, ga_rows):
+        wait_for(grams.at[0, pl.ds(0, gz_rows)], gz_send)
+        wait_for(grams.at[0, pl.ds(0, ga_rows)], ga_send)
+
+    others = z_devices - 1
+    either(
+        z == 0,
+        lambda: own_sent(others * g_part, others * (g_part + 8)),
+        lambda: own_sent(others * g_part + 8, others * g_part),
+    )
     wait_for(grams.at[0], across_send)
     for n, (edge, copy) in enumerate(((is_last, x_up), (is_first, x_down))):
 
@@ -297,7 +330,8 @@
     rows, width = x.shape
     half = width // 2
     dma = pltpu.SemaphoreType.DMA
-    g_half, c_half = 3 * half // 2, width // 2
+    g_half, c_half = half + 8, width // 2
+    g_part = half // z_devices + 8
     others = z_devices - 1
     vmem = lambda *shape: pltpu.VMEM(shape, jnp.float32)
     return pl.pallas_call(
@@ -307,8 +341,8 @@
         out_specs=pl.BlockSpec(memory_space=pltpu.VMEM),
         scratch_shapes=[
             vmem(rows, width), vmem(2, rows, width),
-            vmem(3 * half, half), vmem(g_half, half), vmem(g_half, half),
-            vmem(others, g_half // z_devices, half), vmem(g_half, half), vmem(2, 3 * half, half),
+            vmem(2 * g_half, half), vmem(g_half, half), vmem(g_half, half),
+            vmem(others, g_part, half), vmem(g_part, half), vmem(g_half, half), vmem(2, 2 * g_half, half),
             vmem(c_half, width), vmem(c_half, width), vmem(c_half, width),
             vmem(others, c_half // z_devices, width), vmem(c_half // z_devices, width), vmem(c_half, width),
             vmem(half, half), vmem(half, half),

time: 36.3 us -> 36.1 us (level)
  the two profiles are of different devices: /device:TPU:49 before, /device:TPU:33 now
where the time goes in v5:
time: 36.1 us; the launch traced here: 35.9 us
  Pallas kernels  35.2 us (98%)
  local copies, waits for them, and re-layouts  0.71 us (2%)
    pallas_call x1, Pallas kernels, shards(): pl.pallas_call(functools.partial(kernel, blk_devices, z_devices), out_sha...  35.2 us

profile of v5, /device:TPU:33, one launch (start us, length us, event | category | flops | bytes accessed | tf_op | source)
XLA Modules:
  0.0 35.9 jit_solution(9868246503130735325)
XLA Ops:
  0.0 35.2 %rotate_pairs.1 = f32[256,256]{1,0:T(8,128)S(1)} custom-call(f32[256,256]{1,0:T(8,128)} %x_hbm.1), custom_call_target="tpu_custom_call" | custom-call | flops 4026531840 | bytes 524288 | tf_op jit(solution)/shard_map/rotate_pairs/pallas_call | solution.py:337
  35.2 0.7 %copy.3 = f32[256,256]{1,0:T(8,128)} copy(f32[256,256]{1,0:T(8,128)S(1)} %rotate_pairs.1) | data formatting | bytes 524288

commit v6 on v5

--- a/solution.py
+++ b/solution.py
@@ -136,17 +136,8 @@
     for t in range(z_devices - 1, 0, -1):
         pl.when(z + t < z_devices)(functools.partial(signal, barrier, peer(k, t)))
     neighbours = 2 - is_first.astype(jnp.int32) - is_last.astype(jnp.int32)
+
     load.wait()
-    pl.semaphore_wait(barrier, z + 1 + 2 * neighbours)
-
-    x_up = remote(x_ref, moved.at[up_slot], x_send.at[0], x_recv.at[up_slot], peer(up, 0))
-    x_down = remote(x_ref, moved.at[down_slot], x_send.at[1], x_recv.at[down_slot], peer(down, 0))
-    either(is_last, pltpu.make_async_copy(x_ref, moved.at[1], x_recv.at[1]).start, x_up.start)
-    either(is_first, pltpu.make_async_copy(x_ref, moved.at[0], x_recv.at[0]).start, x_down.start)
-
-    for t in range(z_devices - 1, 0, -1):
-        pl.when(z - t >= 0)(functools.partial(signal, here_sem.at[t - 1], peer(k, z_devices - t)))
-
     x_split = split(x_ref[...])
     g = dot3(x_split, x_split, 0)
     block_rows = lax.broadcasted_iota(jnp.int32, (half_width, half_width), 0)
@@ -158,8 +149,19 @@
     )
     gram_local[g_half + half_width :] = jnp.broadcast_to(diagonals(g[half_width:, half_width:])[1], (8, half_width))
 
+    pl.semaphore_wait(barrier, z + 1 + 2 * neighbours)
+
+    for t in range(z_devices - 1, 0, -1):
+        pl.when(z - t >= 0)(functools.partial(signal, here_sem.at[t - 1], peer(k, z_devices - t)))
+
     gc = remote(gram_local.at[rows_at((1 - core) * g_half, g_half)], gram_core, gc_send, gc_recv, sibling)
     gc.start()
+
+    x_up = remote(x_ref, moved.at[up_slot], x_send.at[0], x_recv.at[up_slot], peer(up, 0))
+    x_down = remote(x_ref, moved.at[down_slot], x_send.at[1], x_recv.at[down_slot], peer(down, 0))
+    either(is_last, pltpu.make_async_copy(x_ref, moved.at[1], x_recv.at[1]).start, x_up.start)
+    either(is_first, pltpu.make_async_copy(x_ref, moved.at[0], x_recv.at[0]).start, x_down.start)
+
 
     def to_others(src, dst, send, recv):
         for there in range(z_devices):
@@ -197,20 +199,29 @@
         pltpu.make_async_copy(src, dst, sem).start()
         to_others(src, dst, ga_send, sem)
 
+    cc = remote(cross_local, cross_core, cc_send, cc_recv, sibling)
+
+    def gram_sum_part():
+        either(
+            z == 0,
+            functools.partial(own_part, *g_parts[0]),
+            lambda: own_part(pl.multiple_of(8 + z * g_part, 8), g_part),
+        )
+
+    def cross_part():
+        for slot in range(2):
+            wait_for(moved.at[slot], x_recv.at[slot])
+        b_split = split(moved[1])
+        a_half = [half_of(moved[0], core == which, 1) for which in (0, 1)]
+        cross_local[...] = dot3(split(a_half[0]), b_split, 0)
+        cc.start()
+        cross_sum[...] = dot3(split(a_half[1]), b_split, 0)
     either(
-        z == 0,
-        functools.partial(own_part, *g_parts[0]),
-        lambda: own_part(pl.multiple_of(8 + z * g_part, 8), g_part),
-    )
-
-    for slot in range(2):
-        wait_for(moved.at[slot], x_recv.at[slot])
-    b_split = split(moved[1])
-    a_half = [half_of(moved[0], core == which, 1) for which in (0, 1)]
-    cross_local[...] = dot3(split(a_half[0]), b_split, 0)
-    cc = remote(cross_local, cross_core, cc_send, cc_recv, sibling)
-    cc.start()
-    cross_sum[...] = dot3(split(a_half[1]), b_split, 0)
+        lower_side,
+        lambda: (cross_part(), gram_sum_part()),
+        lambda: (gram_sum_part(), cross_part()),
+    )
+
     cc.wait_recv()
     cross_sum[...] += cross_core[...]
     for t in far_first:

time: 36.1 us -> 36.1 us (level)
  no operation moved by 1% of the time
where the time goes in v6:
time: 36.1 us; the launch traced here: 36 us
  Pallas kernels  35.2 us (98%)
  local copies, waits for them, and re-layouts  0.71 us (2%)
    pallas_call x1, Pallas kernels, shards(): pl.pallas_call(functools.partial(kernel, blk_devices, z_devices), out_sha...  35.2 us

profile of v6, /device:TPU:33, one launch (start us, length us, event | category | flops | bytes accessed | tf_op | source)
XLA Modules:
  0.0 36.0 jit_solution(17268868097609488582)
XLA Ops:
  0.0 35.2 %rotate_pairs.1 = f32[256,256]{1,0:T(8,128)S(1)} custom-call(f32[256,256]{1,0:T(8,128)} %x_hbm.1), custom_call_target="tpu_custom_call" | custom-call | flops 4026531840 | bytes 524288 | tf_op jit(solution)/shard_map/rotate_pairs/pallas_call | solution.py:348
  35.3 0.7 %copy.3 = f32[256,256]{1,0:T(8,128)} copy(f32[256,256]{1,0:T(8,128)S(1)} %rotate_pairs.1) | data formatting | bytes 524288

commit v7 on v6

--- a/solution.py
+++ b/solution.py
@@ -224,9 +224,13 @@
 
     cc.wait_recv()
     cross_sum[...] += cross_core[...]
-    for t in far_first:
-        there = rows_at(lax.rem(z + t, z_devices) * c_part, c_part)
-        remote(cross_sum.at[there], cross_parts.at[t - 1], cz_send, cz_recv, peer(k, t)).start()
+    for owner in sorted(range(z_devices), key=lambda n: -min(n, z_devices - n)):
+        t = lax.rem(owner - z + z_devices, z_devices)
+        copy = remote(
+            cross_sum.at[pl.ds(owner * c_part, c_part)], cross_parts.at[jnp.maximum(t - 1, 0)], cz_send, cz_recv,
+            {"blk": k, "row": owner * 2 + core},
+        )
+        pl.when(z != owner)(copy.start)
 
     def forward(side):
         start = g_parts[side * middle][0]

time: 36.1 us -> 36 us (level)
  no operation moved by 1% of the time
where the time goes in v7:
time: 36 us; the launch traced here: 35.8 us
  Pallas kernels  35.1 us (98%)
  local copies, waits for them, and re-layouts  0.71 us (2%)
    pallas_call x1, Pallas kernels, shards(): pl.pallas_call(functools.partial(kernel, blk_devices, z_devices), out_sha...  35.1 us

profile of v7, /device:TPU:33, one launch (start us, length us, event | category | flops | bytes accessed | tf_op | source)
XLA Modules:
  0.0 35.8 jit_solution(3872142545762562738)
XLA Ops:
  0.0 35.1 %rotate_pairs.1 = f32[256,256]{1,0:T(8,128)S(1)} custom-call(f32[256,256]{1,0:T(8,128)} %x_hbm.1), custom_call_target="tpu_custom_call" | custom-call | flops 4026531840 | bytes 524288 | tf_op jit(solution)/shard_map/rotate_pairs/pallas_call | solution.py:352
  35.1 0.7 %copy.3 = f32[256,256]{1,0:T(8,128)} copy(f32[256,256]{1,0:T(8,128)S(1)} %rotate_pairs.1) | data formatting | bytes 524288

commit v8 on v7

--- a/solution.py
+++ b/solution.py
@@ -30,8 +30,8 @@
     half = high.shape[0] // 2
     blocks = []
     for rows in (slice(0, half), slice(half, 2 * half)):
-        small = product(high[rows], b[1]) + product(low[rows], b[0])
-        blocks.append(product(high[rows], b[0]) + small)
+        both = product(jnp.concatenate([high[rows], low[rows]], axis=0), b[0])
+        blocks.append(both[:half] + (both[half:] + product(high[rows], b[1])))
     return jnp.concatenate(blocks, axis=0)
 
 

time: 36 us -> 35.9 us (level)
  no operation moved by 1% of the time
where the time goes in v8:
time: 35.9 us; the launch traced here: 35.8 us
  Pallas kernels  35.1 us (98%)
  local copies, waits for them, and re-layouts  0.71 us (2%)
    pallas_call x1, Pallas kernels, shards(): pl.pallas_call(functools.partial(kernel, blk_devices, z_devices), out_sha...  35.1 us

profile of v8, /device:TPU:33, one launch (start us, length us, event | category | flops | bytes accessed | tf_op | source)
XLA Modules:
  0.0 35.8 jit_solution(61389659419596694)
XLA Ops:
  0.0 35.1 %rotate_pairs.1 = f32[256,256]{1,0:T(8,128)S(1)} custom-call(f32[256,256]{1,0:T(8,128)} %x_hbm.1), custom_call_target="tpu_custom_call" | custom-call | flops 4026531840 | bytes 524288 | tf_op jit(solution)/shard_map/rotate_pairs/pallas_call | solution.py:352
  35.1 0.7 %copy.3 = f32[256,256]{1,0:T(8,128)} copy(f32[256,256]{1,0:T(8,128)S(1)} %rotate_pairs.1) | data formatting | bytes 524288

commit v9 on v8

--- a/solution.py
+++ b/solution.py
@@ -26,7 +26,9 @@
 def dot3(a, b, lhs_dim=1):
     high, low = a
     if lhs_dim == 0:
-        return product(high, b[0], 0) + (product(high, b[1], 0) + product(low, b[0], 0))
+        n = high.shape[1]
+        both = product(jnp.concatenate([high, low], axis=1), b[0], 0)
+        return both[:n] + (both[n:] + product(high, b[1], 0))
     half = high.shape[0] // 2
     blocks = []
     for rows in (slice(0, half), slice(half, 2 * half)):

time: 35.9 us -> 35.9 us (level)
  no operation moved by 1% of the time
where the time goes in v9:
time: 35.9 us; the launch traced here: 35.8 us
  Pallas kernels  35.1 us (98%)
  local copies, waits for them, and re-layouts  0.71 us (2%)
    pallas_call x1, Pallas kernels, shards(): pl.pallas_call(functools.partial(kernel, blk_devices, z_devices), out_sha...  35.1 us

profile of v9, /device:TPU:33, one launch (start us, length us, event | category | flops | bytes accessed | tf_op | source)
XLA Modules:
  0.0 35.8 jit_solution(398862184117616286)
XLA Ops:
  0.0 35.1 %rotate_pairs.1 = f32[256,256]{1,0:T(8,128)S(1)} custom-call(f32[256,256]{1,0:T(8,128)} %x_hbm.1), custom_call_target="tpu_custom_call" | custom-call | flops 4026531840 | bytes 524288 | tf_op jit(solution)/shard_map/rotate_pairs/pallas_call | solution.py:354
  35.1 0.7 %copy.3 = f32[256,256]{1,0:T(8,128)} copy(f32[256,256]{1,0:T(8,128)S(1)} %rotate_pairs.1) | data formatting | bytes 524288
